TPU v7x, 128 devices: a whole 4x4x4 slice. The times are simulated.
128 devices in a mesh: blk: 32 (over x, y, z_lo), rep: 4 (over z_hi, core).
Axes of the slice: x: 4, y: 4, z: 4 (z_hi: 2, z_lo: 2; z = z_hi * 2 + z_lo), core: 2. Of those that a mesh axis runs over, the one named last changes fastest.
Arguments:
- tile_values: bfloat16 [32, 4, 32, 1, 256, 256], P('blk', 'rep'), may hold values from -0.1875 to 0.1875
- tile_rows: int32 [32, 4, 32, 1], P('blk', 'rep'), may hold values from 0 to 1, as said below
- tile_cols: int32 [32, 4, 32, 1], P('blk', 'rep'), may hold values from 0 to 1
- tile_counts: int32 [32, 4, 32], P('blk', 'rep'), may hold values from 0 to 1, as said below
- grad_out: bfloat16 [16384, 512], P('blk'), may hold values from -6 to 6
- features: bfloat16 [16384, 512], P(('blk', 'rep')), may hold values from -0.125 to 0.125
- weight: bfloat16 [512, 512], replicated, may hold values from -0.25 to 0.25
Outputs:
- grad_features: float32 [16384, 512], P(('blk', 'rep'))
- grad_weight: float32 [512, 512], replicated
Inputs may be any that keep to these rules, and one draw needn't show every extreme that they name: `tile_counts`: every device has some column block with all 1 slots used. `tile_rows`: for each row block and column block, the slots of all devices of that row block lie at distinct tile positions.
All inputs are finite; a program needn't handle non-finite values.
Results may differ from a plain program's by a relative error of at most 0.0029.
Values may be sent and summed in bfloat16 or wider, within the bound.
A program may use at most 128 MiB of HBM per device.

v0:
```python
import jax
import jax.numpy as jnp
from jax import lax
from jax.sharding import PartitionSpec as P


def block_terms(values_here, selected, col_idx, count_here, per_row):
    product = jnp.einsum(
        "jsab,jsaf->jsbf", values_here, selected, preferred_element_type=jnp.float32
    )
    slot_iota = jnp.arange(values_here.shape[1])[None, :]
    valid = (slot_iota < count_here[:, None]).astype(jnp.float32)
    place = (col_idx[..., None] == jnp.arange(per_row)[None, None, :]).astype(jnp.float32) * valid[
        ..., None
    ]
    return jnp.einsum("jsc,jsbf->jcbf", place, product, precision=lax.Precision.HIGHEST)


def body(tile_values, tile_rows, tile_cols, tile_counts, grad_out, features, weight):
    values_here = tile_values[0, 0]
    row_idx = tile_rows[0, 0]
    col_idx = tile_cols[0, 0]
    count_here = tile_counts[0, 0]
    tile_side = values_here.shape[-1]
    blk_rows = grad_out.shape[0]
    width = grad_out.shape[1]
    per_row = blk_rows // tile_side
    g_flat = grad_out.reshape(per_row, tile_side, width)
    selected = g_flat[row_idx]
    term = block_terms(values_here, selected, col_idx, count_here, per_row)
    own_block = lax.psum_scatter(
        term.reshape(blk_rows * lax.axis_size("blk"), width), "blk", scatter_dimension=0, tiled=True
    )
    shared = lax.psum_scatter(own_block, "rep", scatter_dimension=0, tiled=True)
    rounded = shared.astype(jnp.bfloat16)
    grad_features = lax.dot_general(
        rounded, weight, (((1,), (1,)), ((), ())), preferred_element_type=jnp.float32
    )
    partial_weight = lax.dot_general(
        features, rounded, (((0,), (0,)), ((), ())), preferred_element_type=jnp.float32
    )
    grad_weight = lax.psum(partial_weight, ("blk", "rep"))
    return (grad_features, grad_weight)


def solution(mesh):
    placed = (
        P("blk", "rep", None, None, None, None),
        P("blk", "rep", None, None),
        P("blk", "rep", None, None),
        P("blk", "rep", None),
        P("blk", None),
        P(("blk", "rep"), None),
        P(),
    )
    return jax.shard_map(
        body, mesh=mesh, in_specs=placed, out_specs=(P(("blk", "rep"), None), P()), check_vma=False
    )
```

profile of v0, /device:TPU:1, one launch (start us, length us, event | category | flops | bytes accessed | tf_op | source)
XLA Modules:
  0.0 972.1 jit_solution(8976167498495208583)
XLA Ops:
  7.2 0.0 copy-start
  7.2 0.0 reduce-scatter.3.cloned.1.call-start
  7.2 0.7 fusion.6
  7.9 0.7 fusion.5
  8.6 0.0 copy-done
  8.6 4.9 gather_fusion
  13.5 12.7 %convolution_bitcast_fusion = f32[32,256,512]{1,2,0:T(8,128)} fusion(bf16[32,256,512]{2,1,0:T(8,128)(2,1)} %gather_fusion, bf16[1,1,32,1,256,256]{5,4,3,2,1,0:T(8,128)(2,1)} %param.7), kind=kOutput, calls=%fused_computation.2 | convolution fusion | flops 2147483648 | bytes 29360128 | tf_op jit(solution)/shard_map/jsab,jsaf->jsbf/dot_general | solution.py:8
  26.3 17.5 %copy.12 = f32[32,256,512]{2,1,0:T(8,128)} copy(f32[32,256,512]{1,2,0:T(8,128)} %convolution_bitcast_fusion) | data formatting | bytes 33554432 | tf_op jit(solution)/shard_map/jsab,jsaf->jsbf/dot_general | solution.py:8
  43.7 0.0 copy-done.4
  43.7 0.1 fusion.4
  43.8 19.0 %broadcast_multiply_fusion = f32[32,2,256,512]{3,2,1,0:T(8,128)} fusion(f32[32,256,512]{2,1,0:T(8,128)} %copy.12, f32[32,2]{1,0:T(8,128)S(1)} %fusion.4), kind=kLoop, calls=%fused_computation.1 | loop fusion | flops 8388608 | bytes 50331904 | tf_op jit(solution)/shard_map/jsc,jsbf->jcbf/dot_general | solution.py:16
  62.8 0.0 reduce-scatter.3.cloned.1.call-update
  62.8 0.0 copy-start.1
  62.8 0.0 reduce-scatter.5.cloned.1.call-start
  62.9 711.8 %reduce-scatter.3.cloned.1.call-done = f32[512,512]{1,0:T(8,128)} async-done(((f32[16384,512]{1,0:T(8,128)}), f32[512,512]{1,0:T(8,128)}) %reduce-scatter.3.cloned.1.call-update) | async-done | bytes 1048592 | tf_op jit(solution)/shard_map/reduce_scatter | solution.py:31
  774.7 0.0 reduce-scatter.5.cloned.1.call-update
  774.7 0.0 all-reduce.2.cloned.1.call-start
  774.8 35.5 %reduce-scatter.5.cloned.1.call-done = f32[128,512]{1,0:T(8,128)} async-done(((f32[512,512]{1,0:T(8,128)}), f32[128,512]{1,0:T(8,128)}) %reduce-scatter.5.cloned.1.call-update) | async-done | bytes 262160 | tf_op jit(solution)/shard_map/reduce_scatter | solution.py:34
  810.3 0.0 copy-done.3
  810.3 2.2 convolution_bitcast_fusion.1
  812.5 0.0 all-reduce.2.cloned.1.call-update
  812.5 2.0 fusion.2
  814.5 148.5 %all-reduce.2.cloned.1.call-done = f32[512,512]{0,1:T(8,128)} async-done(((f32[512,512]{0,1:T(8,128)}), f32[512,512]{0,1:T(8,128)}) %all-reduce.2.cloned.1.call-update) | async-done | bytes 1048592 | tf_op jit(solution)/shard_map/psum | solution.py:42
  963.0 2.5 copy.13
  (6 shorter events, 0.0 us)
Async XLA Ops:
  7.2 1.4 copy-start
  7.2 767.5 %reduce-scatter.3.cloned.1.call-start = ((), (), s32[]{:S(2)}) async-start(), calls=%async_computation.2 | async-start | bytes 34603008 | tf_op jit(solution)/shard_map/reduce_scatter | solution.py:31
  26.3 17.5 %copy-start.4 = (s32[1,1,32,1]{2,3,1,0:T(1,128)S(1)}, s32[1,1,32,1]{2,3,1,0:T(1,128)}, u32[]{:S(2)}) copy-start(s32[1,1,32,1]{2,3,1,0:T(1,128)} %param.9) | copy-start | bytes 388
  62.8 747.5 %copy-start.3 = (bf16[128,512]{1,0:T(8,128)(2,1)S(1)}, bf16[128,512]{1,0:T(8,128)(2,1)}, u32[]{:S(2)}) copy-start(bf16[128,512]{1,0:T(8,128)(2,1)} %param.12) | copy-start | bytes 393220
  62.8 749.7 %copy-start.2 = (bf16[512,512]{1,0:T(8,128)(2,1)S(1)}, bf16[512,512]{1,0:T(8,128)(2,1)}, u32[]{:S(2)}) copy-start(bf16[512,512]{1,0:T(8,128)(2,1)} %param.13) | copy-start | bytes 1572868
  62.8 902.7 %copy-start.1 = (bf16[512,512]{1,0:T(8,128)(2,1)S(1)}, bf16[512,512]{1,0:T(8,128)(2,1)}, u32[]{:S(2)}) copy-start(bf16[512,512]{1,0:T(8,128)(2,1)} %param.11) | copy-start | bytes 1572868
  62.8 747.4 %reduce-scatter.5.cloned.1.call-start = ((), (), s32[]{:S(2)}) async-start(), calls=%async_computation.3 | async-start | bytes 1310720 | tf_op jit(solution)/shard_map/reduce_scatter | solution.py:34
  774.7 188.2 %all-reduce.2.cloned.1.call-start = ((), (), s32[]{:S(2)}) async-start(), calls=%async_computation.4 | async-start | bytes 2097152 | tf_op jit(solution)/shard_map/psum | solution.py:42
Sparse Core Ops, SparseCore 0:
  63.0 711.7 reduce-scatter.2
  777.4 32.8 reduce-scatter.4
  816.4 146.5 all-reduce.1
where the time goes:
time: 973 us; the launch traced here: 972 us
  waiting for transfers between devices  896 us (92%)
  local copies, waits for them, and re-layouts  24.9 us (3%)
  other arithmetic  20.4 us (2%)
  matrix products  16.9 us (2%)
  between operations  13.8 us (1%)
    reduce_scatter x1, waiting for transfers between devices, body(): lax.psum_scatter(term.reshape(blk_rows * lax.axis_size('blk'), width), 'b...  712 us
    psum x1, waiting for transfers between devices, body(): grad_weight = lax.psum(partial_weight, ('blk', 'rep'))  149 us
    reduce_scatter x1, waiting for transfers between devices, body(): shared = lax.psum_scatter(own_block, 'rep', scatter_dimension=0, tiled=True)  35.5 us
  transfers between devices with their start and end apart: 3, of which 3 were waited for; matrix products, arithmetic and copies ran while one was open for 0% of the time, Pallas kernels for 0%

commit v1 on v0

--- a/solution.py
+++ b/solution.py
@@ -39,7 +39,7 @@
     partial_weight = lax.dot_general(
         features, rounded, (((0,), (0,)), ((), ())), preferred_element_type=jnp.float32
     )
-    grad_weight = lax.psum(partial_weight, ("blk", "rep"))
+    grad_weight = lax.psum(lax.psum(partial_weight, "blk"), "rep")
     return (grad_features, grad_weight)
 
 

time: 973 us -> 1180 us (1.21)
  waiting for transfers between devices: 896 us -> 1100 us
    psum x1 -> x2, waiting for transfers between devices: 149 us -> 356 us  [body(): grad_weight = lax.psum(lax.psum(partial_weight, 'blk'), 'rep')]
  transfers between devices with their start and end apart: 3 -> 4, of which waited for: 3 -> 4; matrix products, arithmetic and copies ran while one was open for 0% -> 0% of each run, Pallas kernels for 0% -> 0%
where the time goes in v1:
time: 1180 us
  waiting for transfers between devices  1100 us (93%)
  local copies, waits for them, and re-layouts  24.9 us (2%)
  other arithmetic  20.4 us (2%)
  matrix products  16.9 us (1%)
  between operations  13.8 us (1%)
    reduce_scatter x1, waiting for transfers between devices, body(): lax.psum_scatter(term.reshape(blk_rows * lax.axis_size('blk'), width), 'b...  712 us
    psum x2, waiting for transfers between devices, body(): grad_weight = lax.psum(lax.psum(partial_weight, 'blk'), 'rep')  356 us
    reduce_scatter x1, waiting for transfers between devices, body(): shared = lax.psum_scatter(own_block, 'rep', scatter_dimension=0, tiled=True)  35.5 us
  transfers between devices with their start and end apart: 4, of which 4 were waited for; matrix products, arithmetic and copies ran while one was open for 0% of the time, Pallas kernels for 0%

profile of v1, /device:TPU:1, one launch (start us, length us, event | category | flops | bytes accessed | tf_op | source)
XLA Modules:
  0.0 1179.1 jit_solution(17238405719259061459)
XLA Ops:
  7.2 0.0 copy-start
  7.2 0.0 reduce-scatter.3.cloned.1.call-start
  7.2 0.7 fusion.6
  7.9 0.7 fusion.5
  8.6 4.9 gather_fusion
  13.5 12.7 %convolution_bitcast_fusion = f32[32,256,512]{1,2,0:T(8,128)} fusion(bf16[32,256,512]{2,1,0:T(8,128)(2,1)} %gather_fusion, bf16[1,1,32,1,256,256]{5,4,3,2,1,0:T(8,128)(2,1)} %param.7), kind=kOutput, calls=%fused_computation.2 | convolution fusion | flops 2147483648 | bytes 29360128 | tf_op jit(solution)/shard_map/jsab,jsaf->jsbf/dot_general | solution.py:8
  26.3 17.5 %copy.12 = f32[32,256,512]{2,1,0:T(8,128)} copy(f32[32,256,512]{1,2,0:T(8,128)} %convolution_bitcast_fusion) | data formatting | bytes 33554432 | tf_op jit(solution)/shard_map/jsab,jsaf->jsbf/dot_general | solution.py:8
  43.7 0.1 fusion.4
  43.8 19.0 %broadcast_multiply_fusion = f32[32,2,256,512]{3,2,1,0:T(8,128)} fusion(f32[32,256,512]{2,1,0:T(8,128)} %copy.12, f32[32,2]{1,0:T(8,128)S(1)} %fusion.4), kind=kLoop, calls=%fused_computation.1 | loop fusion | flops 8388608 | bytes 50331904 | tf_op jit(solution)/shard_map/jsc,jsbf->jcbf/dot_general | solution.py:16
  62.8 0.0 reduce-scatter.3.cloned.1.call-update
  62.8 0.0 copy-start.1
  62.8 0.0 reduce-scatter.5.cloned.1.call-start
  62.9 711.8 %reduce-scatter.3.cloned.1.call-done = f32[512,512]{1,0:T(8,128)} async-done(((f32[16384,512]{1,0:T(8,128)}), f32[512,512]{1,0:T(8,128)}) %reduce-scatter.3.cloned.1.call-update) | async-done | bytes 1048592 | tf_op jit(solution)/shard_map/reduce_scatter | solution.py:31
  774.7 0.0 reduce-scatter.5.cloned.1.call-update
  774.7 0.0 all-reduce.3.cloned.1.call-start
  774.8 35.5 %reduce-scatter.5.cloned.1.call-done = f32[128,512]{1,0:T(8,128)} async-done(((f32[512,512]{1,0:T(8,128)}), f32[128,512]{1,0:T(8,128)}) %reduce-scatter.5.cloned.1.call-update) | async-done | bytes 262160 | tf_op jit(solution)/shard_map/reduce_scatter | solution.py:34
  810.3 2.2 convolution_bitcast_fusion.1
  812.5 0.0 all-reduce.3.cloned.1.call-update
  812.5 0.0 all-reduce.5.cloned.1.call-start
  812.6 287.6 %all-reduce.3.cloned.1.call-done = f32[512,512]{0,1:T(8,128)} async-done(((f32[512,512]{0,1:T(8,128)}), f32[512,512]{0,1:T(8,128)}) %all-reduce.3.cloned.1.call-update) | async-done | bytes 1048592 | tf_op jit(solution)/shard_map/psum | solution.py:42
  1100.2 0.0 all-reduce.5.cloned.1.call-update
  1100.2 2.0 fusion.2
  1102.2 67.9 %all-reduce.5.cloned.1.call-done = f32[512,512]{0,1:T(8,128)} async-done(((f32[512,512]{0,1:T(8,128)}), f32[512,512]{0,1:T(8,128)}) %all-reduce.5.cloned.1.call-update) | async-done | bytes 1048592 | tf_op jit(solution)/shard_map/psum | solution.py:42
  1170.1 2.5 copy.13
  (9 shorter events, 0.0 us)
Async XLA Ops:
  7.2 1.4 copy-start
  7.2 767.5 %reduce-scatter.3.cloned.1.call-start = ((), (), s32[]{:S(2)}) async-start(), calls=%async_computation.2 | async-start | bytes 34603008 | tf_op jit(solution)/shard_map/reduce_scatter | solution.py:31
  26.3 17.5 %copy-start.4 = (s32[1,1,32,1]{2,3,1,0:T(1,128)S(1)}, s32[1,1,32,1]{2,3,1,0:T(1,128)}, u32[]{:S(2)}) copy-start(s32[1,1,32,1]{2,3,1,0:T(1,128)} %param.9) | copy-start | bytes 388
  62.8 747.5 %copy-start.3 = (bf16[128,512]{1,0:T(8,128)(2,1)S(1)}, bf16[128,512]{1,0:T(8,128)(2,1)}, u32[]{:S(2)}) copy-start(bf16[128,512]{1,0:T(8,128)(2,1)} %param.12) | copy-start | bytes 393220
  62.8 1037.4 %copy-start.2 = (bf16[512,512]{1,0:T(8,128)(2,1)S(1)}, bf16[512,512]{1,0:T(8,128)(2,1)}, u32[]{:S(2)}) copy-start(bf16[512,512]{1,0:T(8,128)(2,1)} %param.13) | copy-start | bytes 1572868
  62.8 1109.8 %copy-start.1 = (bf16[512,512]{1,0:T(8,128)(2,1)S(1)}, bf16[512,512]{1,0:T(8,128)(2,1)}, u32[]{:S(2)}) copy-start(bf16[512,512]{1,0:T(8,128)(2,1)} %param.11) | copy-start | bytes 1572868
  62.8 747.4 %reduce-scatter.5.cloned.1.call-start = ((), (), s32[]{:S(2)}) async-start(), calls=%async_computation.3 | async-start | bytes 1310720 | tf_op jit(solution)/shard_map/reduce_scatter | solution.py:34
  774.7 325.5 %all-reduce.3.cloned.1.call-start = ((), (), s32[]{:S(2)}) async-start(), calls=%async_computation.4 | async-start | bytes 2097152 | tf_op jit(solution)/shard_map/psum | solution.py:42
  812.5 357.6 %all-reduce.5.cloned.1.call-start = ((), (), s32[]{:S(2)}) async-start(), calls=%async_computation.5 | async-start | bytes 2097152 | tf_op jit(solution)/shard_map/psum | solution.py:42
Sparse Core Ops, SparseCore 0:
  63.0 711.7 reduce-scatter.2
  777.4 32.8 reduce-scatter.4
  813.5 286.6 all-reduce.2
  1102.6 67.4 all-reduce.4
